TPU v7x, 768 devices: a whole 4x8x12 slice. The times are simulated.
768 devices in a mesh: ctx: 96 (over z, y), head: 8 (over x, core).
Axes of the slice: x: 4, y: 8, z: 12, core: 2. Of those that a mesh axis runs over, the one named last changes fastest.
Arguments:
- text_qkv: bfloat16 [12288, 3, 8192], P('ctx', None, 'head'), may hold values from -6 to 6
- vis_feats: bfloat16 [384, 1024], P('ctx'), may hold values from -6 to 6
- w_visual: bfloat16 [1024, 3, 8192], P(None, None, 'head'), may hold values from -0.1875 to 0.1875
- vis_src: int32 [12288], P('ctx'), may hold values from -1 to 383, as said below
- log_decay: float32 [64, 12288], P('head', 'ctx'), as said below
- norm_gain: float32 [8192], P('head'), may hold values from 0.5 to 1.5
Outputs:
- attn_out: bfloat16 [12288, 8192], P('ctx', 'head')
Inputs may be any that keep to these rules, and one draw needn't show every extreme that they name: `vis_src`: -1 marks a text position; any other value is the row of vis_feats placed at that position; each of the 384 rows is placed at exactly one position; positions 0 and 1 are visual and take the rows 192 and 383; the later visual positions, in order along the sequence, take the rows 193 to 382 and then 0 to 191. `log_decay`: at most 0; differs from position to position.
All inputs are finite; a program needn't handle non-finite values.
Results may differ from a plain program's by a relative error of at most 0.0034.
Values may be sent and summed in bfloat16 or wider, within the bound.
A program may use at most 128 MiB of HBM per device.

v0:
```python
import jax
import jax.numpy as jnp
from jax import lax
from jax.sharding import PartitionSpec as P


def entering_2(x, axis, combine, identity):
    count, index = (lax.axis_size(axis), lax.axis_index(axis))
    everything = jax.tree.map(lambda part: lax.all_gather(part, axis), x)
    start = jax.tree.map(
        lambda part, zero: jnp.broadcast_to(jnp.asarray(zero, part.dtype), part.shape), x, identity
    )

    def step(k, before):
        reached = k < index
        new = combine(before, jax.tree.map(lambda part: part[k], everything))
        return jax.tree.map(lambda a, b: jnp.where(reached, a, b), new, before)

    return lax.fori_loop(0, count, step, start)


def place_rows(vis_src):

    def placer(current, arrived, first_row):
        arrived_count = arrived.shape[0]
        inside = (vis_src >= 0) & (vis_src < arrived_count)
        taken = jnp.take(arrived, jnp.clip(vis_src, 0, arrived_count - 1), axis=0)
        return jnp.where(inside[:, None], taken, current)

    return placer


def combine(before_part, after_part):
    return (
        before_part[0] + after_part[0],
        jnp.exp(after_part[0])[:, None, None] * before_part[1] + after_part[1],
    )


def local(text_qkv, vis_feats, w_visual, vis_src, log_decay, norm_gain):
    highest = lax.Precision.HIGHEST
    row_count = text_qkv.shape[0]
    inner_dev = text_qkv.shape[2]
    head_count = log_decay.shape[0]
    head_size = inner_dev // head_count
    feature_width = vis_feats.shape[1]
    flat_weight = w_visual.reshape(w_visual.shape[0], 3 * inner_dev)
    placer = place_rows(vis_src)
    blank_rows = jnp.zeros((row_count, feature_width), jnp.bfloat16)
    placed = placer(blank_rows, lax.all_gather(vis_feats, "ctx", axis=0, tiled=True), jnp.int32(0))
    visual_qkv = jnp.dot(placed, flat_weight, preferred_element_type=jnp.float32).astype(
        jnp.bfloat16
    )
    visual_qkv = visual_qkv.reshape(row_count, 3, inner_dev)
    all_qkv = jnp.where((vis_src >= 0)[:, None, None], visual_qkv, text_qkv)
    query_rows = all_qkv[:, 0].reshape(row_count, head_count, head_size)
    key_rows = all_qkv[:, 1].reshape(row_count, head_count, head_size)
    value_rows = all_qkv[:, 2].reshape(row_count, head_count, head_size)
    cumulative = jnp.cumsum(log_decay, axis=1)
    causal = jnp.arange(row_count)[:, None] >= jnp.arange(row_count)[None, :]
    scores = jnp.einsum("shd,thd->hst", query_rows, key_rows, preferred_element_type=jnp.float32)
    decay_gap = jnp.where(causal[None], cumulative[:, :, None] - cumulative[:, None, :], -jnp.inf)
    weights = (scores * jnp.exp(decay_gap)).astype(jnp.bfloat16)
    within = jnp.einsum("hst,thd->shd", weights, value_rows, preferred_element_type=jnp.float32)
    block_total = cumulative[:, -1]
    scaled_keys = (
        key_rows.astype(jnp.float32) * jnp.exp(block_total[:, None] - cumulative).T[:, :, None]
    )
    local_state = jnp.einsum(
        "thd,the->hde", scaled_keys, value_rows.astype(jnp.float32), precision=highest
    )
    identity = (
        jnp.zeros((head_count,), jnp.float32),
        jnp.zeros((head_count, head_size, head_size), jnp.float32),
    )
    _, entering = entering_2((block_total, local_state), "ctx", combine, identity)
    from_state = jnp.exp(cumulative).T[:, :, None] * jnp.einsum(
        "shd,hde->she", query_rows.astype(jnp.float32), entering, precision=highest
    )
    mixed_out = (within + from_state).reshape(row_count, inner_dev)
    square_sum = lax.psum(jnp.sum(mixed_out * mixed_out, axis=1), "head")
    inverse_rms = lax.rsqrt(square_sum / (inner_dev * lax.axis_size("head")) + 1e-05)
    return (mixed_out * inverse_rms[:, None] * norm_gain).astype(jnp.bfloat16)


def solution(mesh):
    placed = (
        P("ctx", None, "head"),
        P("ctx", None),
        P(None, None, "head"),
        P("ctx"),
        P("head", "ctx"),
        P("head"),
    )
    return jax.shard_map(
        local, mesh=mesh, in_specs=placed, out_specs=P("ctx", "head"), check_vma=False
    )
```

profile of v0, /device:TPU:1, one launch (start us, length us, event | category | flops | bytes accessed | tf_op | source)
XLA Modules:
  0.0 589.9 jit_solution(8101298657832813860)
XLA Ops:
  7.2 67.9 %all-gather.2 = bf16[96,4,1024]{2,1,0:T(4,128)(2,1)S(1)} all-gather(bf16[1,4,1024]{2,1,0:T(4,128)(2,1)} %bitcast.48), channel_id=1, replica_groups=mesh['ctx'=96,'head'=8] {'ctx'}, dimensions={0}, use_global_device_ids=true | all-gather | bytes 794624 | tf_op jit(solution)/shard_map/all_gather | solution.py:50
  75.3 8.7 %copy.29 = bf16[1024,3,1024]{0,2,1:T(8,128)(2,1)} copy(bf16[1024,3,1024]{2,0,1:T(8,128)(2,1)} %param.10) | data formatting | bytes 12582912 | tf_op args[2]
  84.8 5.0 convolution_convert_fusion
  91.3 1.5 fusion.4
  92.8 1.3 dynamic-slice
  95.0 169.8 %all-reduce = f32[768]{0:T(1024)S(1)} all-reduce(f32[768]{0:T(1024)S(1)} %dynamic-update-slice), channel_id=2, replica_groups=mesh['ctx'=96,'head'=8] {'ctx'}, use_global_device_ids=true, to_apply=%add | all-reduce | flops 768 | bytes 6144
  264.9 186.3 %all-gather.5.cloned.1.call-done = f32[768,128,128]{2,1,0:T(8,128)} async-done(((f32[8,128,128]{2,1,0:T(8,128)}), f32[768,128,128]{2,1,0:T(8,128)}) %all-gather.5.cloned.1.call-update) | async-done | bytes 50331664 | tf_op jit(solution)/shard_map/all_gather | solution.py:9
  451.2 116.6 %while.14 = (s32[]{:T(128)}, f32[8,128,128]{2,1,0:T(8,128)S(1)}, s32[]{:T(128)}, f32[96,8]{1,0:T(8,128)S(1)}, f32[96,8,128,128]{3,2,1,0:T(8,128)}, /*index=5*/s32[]{:T(128)}, s32[]{:T(128)}) while((s32[]{:T(128)}, f32[8,128,128]{2,1,0:T(8,128)S(1)}, s32[]{:T(128)}, f32[96,8]{1,0:T(8,128)S(1)}, f32[96,8,128,128]{3,2,1,0:T(8,128)}, ...), condition=%wide.region_2.3_spmd.clone, body=%wide.region_1.2_spmd.clone.sunk | while | flops 524292 | bytes 1573065 | solution.py:19
  451.2 1.2 fusion.33
  453.6 1.2 fusion.33
  454.8 1.2 fusion.33
  456.0 1.2 fusion.33
  457.2 1.2 fusion.33
  460.9 1.2 fusion.33
  462.1 1.2 fusion.33
  463.3 1.2 fusion.33
  464.5 1.2 fusion.33
  469.4 1.2 fusion.33
  470.6 1.2 fusion.33
  471.8 1.2 fusion.33
  476.7 1.2 fusion.33
  477.9 1.2 fusion.33
  479.1 1.2 fusion.33
  480.3 1.2 fusion.33
  484.0 1.2 fusion.33
  485.2 1.2 fusion.33
  486.4 1.2 fusion.33
  487.6 1.2 fusion.33
  492.5 1.2 fusion.33
  493.7 1.2 fusion.33
  494.9 1.2 fusion.33
  569.1 13.1 %psum.7 = f32[128]{0:T(128)S(1)} all-reduce(f32[128]{0:T(128)S(1)} %get-tuple-element.137), channel_id=1, replica_groups=mesh['ctx'=96,'head'=8] {'head'}, use_global_device_ids=true, to_apply=%region_4.5 | all-reduce | flops 128 | bytes 1024 | tf_op jit(solution)/shard_map/psum | solution.py:81
  (198 shorter events, 92.4 us)
Async XLA Ops:
  6.5 444.6 %all-gather.5.cloned.1.call-start = ((), (), s32[]{:S(2)}) async-start(), calls=%async_computation | async-start | bytes 50855936 | tf_op jit(solution)/shard_map/all_gather | solution.py:9
  83.9 6.3 %copy-start = (bf16[128,3,1024]{2,0,1:T(8,128)(2,1)S(1)}, bf16[128,3,1024]{2,0,1:T(8,128)(2,1)}, u32[]{:S(2)}) copy-start(bf16[128,3,1024]{2,0,1:T(8,128)(2,1)} %param.8) | copy-start | bytes 2359300
  84.8 5.9 %copy-start.2 = (f32[8,128]{1,0:T(8,128)S(1)}, f32[8,128]{1,0:T(8,128)}, u32[]{:S(2)}) copy-start(f32[8,128]{1,0:T(8,128)} %param.12) | copy-start | bytes 12292
  92.8 489.5 %copy-start.1 = (f32[1024]{0:T(1024)S(1)}, f32[1024]{0:T(1024)}, u32[]{:S(2)}) copy-start(f32[1024]{0:T(1024)} %param.13) | copy-start | bytes 12292
Sparse Core Ops, SparseCore 0:
  92.9 358.2 all-gather.4
where the time goes:
time: 595 us; the launch traced here: 590 us
  blocking collectives  251 us (42%)
  waiting for transfers between devices  186 us (31%)
  other arithmetic  115 us (19%)
  between operations  14.2 us (2%)
  local copies, waits for them, and re-layouts  13.6 us (2%)
  matrix products  7.6 us (1%)
    all_gather x1, waiting for transfers between devices, entering_2(): everything = jax.tree.map(lambda part: lax.all_gather(part, axis), x)  186 us
    unnamed x1, blocking collectives  170 us
    select_n x96, other arithmetic, step(): return jax.tree.map(lambda a, b: jnp.where(reached, a, b), new, before)  113 us
    all_gather x1, blocking collectives, local(): lax.all_gather(vis_feats, 'ctx', axis=0, tiled=True)  67.9 us
    psum x1, blocking collectives, local(): square_sum = lax.psum(jnp.sum(mixed_out * mixed_out, axis=1), 'head')  13.1 us
  transfers between devices with their start and end apart: 1, of which 1 were waited for; matrix products, arithmetic and copies ran while one was open for 0% of the time, Pallas kernels for 0%

commit v1 on v0

v1 whole, which is shorter than its diff:
```python
import functools

import jax
import jax.numpy as jnp
from jax import lax
from jax.experimental import pallas as pl
from jax.experimental.pallas import tpu as pltpu
from jax.sharding import PartitionSpec as P

MESH = pl.DeviceIdType.MESH
F32, BF16 = jnp.float32, jnp.bfloat16
NY = 8
FAR = -1e30
T = 128
TOT_Y, STATE_Y, FEAT_Z, TAB_Y, TOT_Z, FEAT_Y, FEAT_X, FEAT_C, TAB_Z, STATE_Z, BACK_Z, BACK_Y, NORM = range(13)


def dot(a, b, dims=((1,), (0,))):
    return lax.dot_general(a, b, (dims, ((), ())), preferred_element_type=F32)


def lanes(h):
    start = h * T if isinstance(h, int) else pl.multiple_of(h * T, T)
    return pl.ds(start, T)


def kernel(
    nz, nh, heads_total,
    text, feats, w_hbm, vis_src, log_decay, gain, out,
    w, zbuf, x48, fbuf, qkv_vis, qkv, s_out, s_in, e_out, e_in, pstate, t_out, t_in, r_out, r_in,
    tot, tot_z, pre, tab, tab_z, weight, cum, mixed, part, norm, send, recv, w_sem,
):
    nx = nh // 2
    vr = qkv_vis.shape[1]
    zrows = 4 * nz
    owners = t_out.shape[0]
    block_cols = fbuf.shape[3]
    me, hd = lax.axis_index("ctx"), lax.axis_index("head")
    z, y = me // NY, me % NY
    x, core = hd // 2, hd % 2

    def y_dev(to):
        return {"ctx": z * NY + to, "head": hd}

    def z_dev(to):
        return {"ctx": to * NY + y, "head": hd}

    def h_dev(to):
        return {"ctx": me, "head": to}

    def put(src, dst, phase, device):
        pltpu.make_async_remote_copy(
            src_ref=src, dst_ref=dst, send_sem=send.at[phase], recv_sem=recv.at[phase],
            device_id=device, device_id_type=MESH,
        ).start()

    def wait(ref, sem):
        pltpu.make_async_copy(ref, ref, sem).wait()

    def y_peers():
        return [lax.rem(y + k, NY) for k in (4, 3, 5, 2, 6, 1, 7)]

    def z_peers():
        return [lax.rem(z + k, nz) for k in range(1, nz)]

    w_copy = pltpu.make_async_copy(w_hbm, w, w_sem)
    w_copy.start()
    barrier = pltpu.get_barrier_semaphore()
    for to in y_peers():
        pl.semaphore_signal(barrier, inc=1, device_id=y_dev(to), device_id_type=MESH)
    for to in z_peers():
        pl.semaphore_signal(barrier, inc=1, device_id=z_dev(to), device_id_type=MESH)
    for k in range(1, nh):
        pl.semaphore_signal(barrier, inc=1, device_id=h_dev(lax.rem(hd + k, nh)), device_id_type=MESH)

    lane = lax.broadcasted_iota(jnp.int32, (NY, T), 1)
    running = log_decay[...]
    step = 1
    while step < T:
        running = running + jnp.where(lane >= step, pltpu.roll(running, step, 1), 0.0)
        step *= 2
    cum[...] = running
    total = jnp.sum(jnp.where(lane == T - 1, running, 0.0), axis=1, keepdims=True)
    total = jnp.broadcast_to(total, (NY, T))
    tot[y] = total

    source_row = jnp.broadcast_to(vis_src[...], (T, T)).astype(F32)
    source = source_row.T
    is_vis = source >= 0.0
    col = lax.broadcasted_iota(jnp.int32, (1, vr), 1)
    col_y = jnp.zeros((1, vr), jnp.int32)
    for k in range(1, NY):
        col_y = col_y + jnp.where(col >= k * zrows, 1, 0)
    col_z = lax.shift_right_logical(col - col_y * zrows, 2)
    row_id = ((col_z * NY + col_y) * 4 + (col & 3)).astype(F32)
    pick = jnp.concatenate(
        [jnp.where(source == row_id[:, j:j + T], 1.0, 0.0) for j in range(0, vr, T)], axis=1
    ).astype(BF16)

    def head_state(h):
        row = jnp.broadcast_to(cum[pl.ds(h, 1), :], (T, T))
        last = jnp.broadcast_to(tot[y, pl.ds(h, 1), :], (T, T))
        tail = jnp.where(is_vis, 0.0, jnp.exp(last - row.T))
        value = text[2, :, lanes(h)].astype(F32) * tail
        high = value.astype(BF16)
        low = (value - high.astype(F32)).astype(BF16)
        both = dot(text[1, :, lanes(h)], jnp.concatenate([high, low], axis=1), ((0,), (0,)))
        s_out[h] = (both[:, :T] + both[:, T:]).astype(BF16)

    for h in range(NY):
        head_state(h)

    own = feats[...].astype(F32)
    quarter = own.shape[1] // 4
    zbuf[z] = jnp.concatenate([own[:, c * quarter:(c + 1) * quarter] for c in range(4)], axis=0).astype(BF16)

    pl.semaphore_wait(barrier, NY - 1 + nz - 1 + nh - 1)

    for to in y_peers():
        put(tot.at[y], tot.at[y], TOT_Y, y_dev(to))
    for to in y_peers():
        put(s_out.at[to], s_in.at[y], STATE_Y, y_dev(to))
    for to in z_peers():
        put(zbuf.at[z], zbuf.at[z], FEAT_Z, z_dev(to))

    tail = total - running
    high = tail.astype(BF16).astype(F32)
    mid = (tail - high).astype(BF16).astype(F32)
    low = tail - high - mid
    pieces = jnp.concatenate([high, mid, low, jnp.ones_like(tail)], axis=0).astype(BF16)
    table = dot(pieces, pick)
    here = table[3 * NY:] > 0.5
    tab[y] = jnp.where(here, table[:NY] + table[NY:2 * NY] + table[2 * NY:3 * NY], FAR)
    for to in y_peers():
        put(tab.at[y], tab.at[y], TAB_Y, y_dev(to))

    s_in[y] = s_out[y]

    wait(tot.at[pl.ds(0, NY - 1)], recv.at[TOT_Y])
    before = jnp.zeros((NY, T), F32)
    for k in range(NY):
        pre[k] = before
        before = before + tot[k]
    tot_z[z] = before
    for to in z_peers():
        put(tot_z.at[z], tot_z.at[z], TOT_Z, z_dev(to))

    wait(zbuf.at[pl.ds(0, nz - 1)], recv.at[FEAT_Z])
    rows = lax.broadcasted_iota(jnp.int32, (256, 16 * nz), 0)
    folded = lax.broadcasted_iota(jnp.int32, (256, 16 * nz), 1)
    wanted = (lax.shift_right_logical(rows, 2) & 15) * 16 + lax.shift_right_logical(rows, 6) * 4 + (rows & 3)
    unfold = jnp.where(wanted == folded, 1.0, 0.0).astype(BF16)
    unfolded = dot(unfold, zbuf[...].reshape(16 * nz, quarter)).astype(BF16)
    for c in range(4):
        x48[:, c * quarter:(c + 1) * quarter] = unfolded[c * 64:c * 64 + zrows]
    fbuf[hd, y] = x48[:, pl.ds(pl.multiple_of(hd * block_cols, T), block_cols)]
    for to in y_peers():
        put(fbuf.at[hd, y], fbuf.at[hd, y], FEAT_Y, y_dev(to))

    wait(s_in.at[pl.ds(0, NY - 1)], recv.at[STATE_Y])
    state = jnp.zeros((T, T), F32)
    for k in range(NY):
        pstate[k] = state
        state = state * jnp.exp(tot[k, pl.ds(y, 1), :]) + s_in[k].astype(F32)
    share = T // owners
    for i in range(owners):
        t_out[i] = state[i * share:(i + 1) * share]
    for i in range(owners):
        @pl.when(z != i)
        def _():
            put(t_out.at[i], t_in.at[z], STATE_Z, z_dev(i))

    wait(tab.at[pl.ds(0, NY - 1)], recv.at[TAB_Y])

    def wide(a):
        return jnp.concatenate([a] * (vr // T), axis=1)

    row_tab = jnp.full((NY, vr), FAR, F32)
    own_tab = jnp.full((NY, vr), FAR, F32)
    for k in range(NY):
        now = tab[k]
        shift = wide(tot[k])
        row_tab = jnp.maximum(row_tab + shift, now)
        own_tab = jnp.where(k < y, jnp.maximum(own_tab + shift, now), own_tab)
    tab_z[z] = row_tab
    for to in z_peers():
        put(tab_z.at[z], tab_z.at[z], TAB_Z, z_dev(to))

    wait(fbuf.at[0, pl.ds(0, NY - 1)], recv.at[FEAT_Y])
    for k in range(1, nx):
        put(fbuf.at[hd], fbuf.at[hd], FEAT_X, h_dev(lax.rem(x + k, nx) * 2 + core))
    put(fbuf.at[hd], fbuf.at[hd], FEAT_C, h_dev(x * 2 + 1 - core))

    wait(tot_z.at[pl.ds(0, nz - 1)], recv.at[TOT_Z])

    @pl.when(z < owners)
    def _():
        wait(t_in.at[pl.ds(0, nz - 1)], recv.at[STATE_Z])
        t_in[z] = t_out[z]
        carry = jnp.zeros((share, T), F32)
        for k in range(nz):
            r_out[k] = carry
            carry = carry * jnp.exp(tot_z[k, pl.ds(y, 1), :]) + t_in[k]
        for to in z_peers():
            put(r_out.at[to], r_in.at[z], BACK_Z, z_dev(to))
        r_in[z] = r_out[z]

    if nx > 1:
        wait(fbuf.at[pl.ds(0, nx - 1)], recv.at[FEAT_X])
        for k in range(1, nx):
            slab = fbuf.at[lax.rem(x + k, nx) * 2 + core]
            put(slab, slab, FEAT_C, h_dev(x * 2 + 1 - core))

    @pl.when(z < owners)
    def _():
        wait(r_in.at[pl.ds(0, owners - 1)], recv.at[BACK_Z])

    @pl.when(z >= owners)
    def _():
        wait(r_in, recv.at[BACK_Z])

    entering = r_in[...].reshape(T, T)
    for to in y_peers():
        e_out[to] = (pstate[to] + entering * jnp.exp(pre[to, pl.ds(y, 1), :])).astype(BF16)
        put(e_out.at[to], e_in.at[y], BACK_Y, y_dev(to))
    e_in[y] = (pstate[y] + entering * jnp.exp(pre[y, pl.ds(y, 1), :])).astype(BF16)

    wait(tab_z.at[pl.ds(0, nz - 1)], recv.at[TAB_Z])
    far_tab = jnp.full((NY, vr), FAR, F32)
    for k in range(nz):
        far_tab = jnp.where(k < z, jnp.maximum(far_tab + wide(tot_z[k]), tab_z[k]), far_tab)
    weight[...] = jnp.exp(jnp.maximum(far_tab + wide(pre[y]), own_tab))

    wait(fbuf.at[pl.ds(0, nx)], recv.at[FEAT_C])
    w_copy.wait()
    everything = jnp.concatenate([fbuf[k].reshape(vr, block_cols) for k in range(nh)], axis=1)
    chunk = 512
    inner = w.shape[2]

    def project(i, _):
        member, part_of = i // (inner // chunk), i % (inner // chunk)
        cols = pl.ds(pl.multiple_of(part_of * chunk, chunk), chunk)
        qkv_vis[member, :, cols] = dot(everything, w[member, :, cols]).astype(BF16)
        return 0

    lax.fori_loop(0, 3 * (inner // chunk), project, 0)

    causal = lax.broadcasted_iota(jnp.int32, (T, T), 0) >= lax.broadcasted_iota(jnp.int32, (T, T), 1)

    def head_within(h):
        at = lanes(h)
        members = []
        for m in range(3):
            placed = dot(pick, qkv_vis[m, :, at])
            members.append(jnp.where(is_vis, placed, text[m, :, at].astype(F32)).astype(BF16))
        query, key, value = members
        qkv[:, at] = query
        row = jnp.broadcast_to(cum[pl.ds(h, 1), :], (T, T))
        gap = row.T - row
        scores = dot(query, key, ((1,), (1,)))
        weights = jnp.where(causal, scores * jnp.exp(jnp.where(causal, gap, 0.0)), 0.0).astype(BF16)
        mixed[:, at] = dot(weights, value)
        visual = dot(query, qkv_vis[1, :, at], ((1,), (1,))) * weight[pl.ds(h, 1), :]
        part[:, at] = dot(visual.astype(BF16), qkv_vis[2, :, at])

    for h in range(NY):
        head_within(h)

    wait(e_in.at[pl.ds(0, NY - 1)], recv.at[BACK_Y])
    squares = jnp.zeros((T, T), F32)
    for h in range(NY):
        at = lanes(h)
        grown = jnp.exp(jnp.broadcast_to(cum[pl.ds(h, 1), :], (T, T)).T)
        result = mixed[:, at] + grown * (dot(qkv[:, at], e_in[h]) + part[:, at])
        mixed[:, at] = result
        squares = squares + result * result

    norm[hd] = jnp.broadcast_to(jnp.sum(squares.T, axis=0, keepdims=True), (8, T))
    for k in range(1, nh):
        put(norm.at[hd], norm.at[hd], NORM, h_dev(lax.rem(hd + k, nh)))
    wait(norm.at[pl.ds(0, nh - 1)], recv.at[NORM])
    square_sum = norm[0]
    for k in range(1, nh):
        square_sum = square_sum + norm[k]
    inverse = lax.rsqrt(square_sum * (1.0 / heads_total) + 1e-05)
    scale = jnp.broadcast_to(inverse[:1], (T, T)).T
    for h in range(NY):
        at = lanes(h)
        out[:, at] = (mixed[:, at] * scale * gain[:, at]).astype(BF16)

    wait(tot.at[pl.ds(0, NY - 1)], send.at[TOT_Y])
    wait(s_in.at[pl.ds(0, NY - 1)], send.at[STATE_Y])
    wait(zbuf.at[pl.ds(0, nz - 1)], send.at[FEAT_Z])
    wait(tab.at[pl.ds(0, NY - 1)], send.at[TAB_Y])
    wait(tot_z.at[pl.ds(0, nz - 1)], send.at[TOT_Z])
    wait(fbuf.at[0, pl.ds(0, NY - 1)], send.at[FEAT_Y])
    if nx > 1:
        wait(fbuf.at[pl.ds(0, nx - 1)], send.at[FEAT_X])
    wait(fbuf.at[pl.ds(0, nx)], send.at[FEAT_C])
    wait(tab_z.at[pl.ds(0, nz - 1)], send.at[TAB_Z])

    @pl.when(z < owners)
    def _():
        wait(t_out.at[pl.ds(0, owners - 1)], send.at[STATE_Z])
        wait(r_out.at[pl.ds(0, nz - 1)], send.at[BACK_Z])

    @pl.when(z >= owners)
    def _():
        wait(t_out, send.at[STATE_Z])

    wait(e_out.at[pl.ds(0, NY - 1)], send.at[BACK_Y])
    wait(norm.at[pl.ds(0, nh - 1)], send.at[NORM])


def local(nz, nh, text_qkv, vis_feats, w_visual, vis_src, log_decay, norm_gain):
    row_count, _, inner = text_qkv.shape
    width = vis_feats.shape[1]
    vr = vis_feats.shape[0] * NY * nz
    owners = 8 if nz >= 8 else nz
    share = T // owners
    vmem = pl.BlockSpec(memory_space=pltpu.VMEM)
    scratch = [
        pltpu.VMEM((3, width, inner), BF16),
        pltpu.VMEM((nz, 16, width // 4), BF16),
        pltpu.VMEM((4 * nz, width), BF16),
        pltpu.VMEM((nh, NY, 4 * nz, width // nh), BF16),
        pltpu.VMEM((3, vr, inner), BF16),
        pltpu.VMEM((row_count, inner), BF16),
        pltpu.VMEM((NY, T, T), BF16),
        pltpu.VMEM((NY, T, T), BF16),
        pltpu.VMEM((NY, T, T), BF16),
        pltpu.VMEM((NY, T, T), BF16),
        pltpu.VMEM((NY, T, T), F32),
        pltpu.VMEM((owners, share, T), F32),
        pltpu.VMEM((nz, share, T), F32),
        pltpu.VMEM((nz, share, T), F32),
        pltpu.VMEM((owners, share, T), F32),
        pltpu.VMEM((NY, NY, T), F32),
        pltpu.VMEM((nz, NY, T), F32),
        pltpu.VMEM((NY, NY, T), F32),
        pltpu.VMEM((NY, NY, vr), F32),
        pltpu.VMEM((nz, NY, vr), F32),
        pltpu.VMEM((NY, vr), F32),
        pltpu.VMEM((NY, T), F32),
        pltpu.VMEM((row_count, inner), F32),
        pltpu.VMEM((row_count, inner), F32),
        pltpu.VMEM((nh, 8, T), F32),
        pltpu.SemaphoreType.DMA((13,)),
        pltpu.SemaphoreType.DMA((13,)),
        pltpu.SemaphoreType.DMA,
    ]
    return pl.pallas_call(
        functools.partial(kernel, nz, nh, inner * nh),
        out_shape=jax.ShapeDtypeStruct((row_count, inner), BF16),
        in_specs=[vmem, vmem, pl.BlockSpec(memory_space=pl.ANY), vmem, vmem, vmem],
        out_specs=vmem,
        scratch_shapes=scratch,
        compiler_params=pltpu.CompilerParams(
            collective_id=0, has_side_effects=True, vmem_limit_bytes=48 * 1024 * 1024
        ),
        name="lightning",
    )(
        text_qkv.transpose(1, 0, 2),
        vis_feats,
        w_visual.transpose(1, 0, 2),
        vis_src.reshape(1, row_count),
        log_decay,
        norm_gain.reshape(1, inner),
    )


def solution(mesh):
    placed = (
        P("ctx", None, "head"),
        P("ctx", None),
        P(None, None, "head"),
        P("ctx"),
        P("head", "ctx"),
        P("head"),
    )
    nz, nh = mesh.shape["ctx"] // NY, mesh.shape["head"]
    return jax.shard_map(
        functools.partial(local, nz, nh), mesh=mesh, in_specs=placed, out_specs=P("ctx", "head"), check_vma=False
    )
```

time: 595 us -> 60.1 us (0.10)
  blocking collectives: 251 us -> 0 us
  waiting for transfers between devices: 186 us -> 0 us
  other arithmetic: 115 us -> 0 us
  Pallas kernels: 0 us -> 55.3 us
  between operations: 14.2 us -> 0.01 us
  local copies, waits for them, and re-layouts: 13.6 us -> 4.56 us
  matrix products: 7.6 us -> 0 us
    all_gather x1 -> x0, waiting for transfers between devices: 186 us -> none  [entering_2(): everything = jax.tree.map(lambda part: lax.all_gather(part, axis), x)]
    unnamed x1 -> x0, blocking collectives: 170 us -> none
    select_n x97 -> x0, other arithmetic: 113 us -> none  [the longest x96 113 us: step(): return jax.tree.map(lambda a, b: jnp.where(reached, a, b), new, before)]
    all_gather x1 -> x0, blocking collectives: 67.9 us -> none  [local(): lax.all_gather(vis_feats, 'ctx', axis=0, tiled=True)]
    pallas_call x0 -> x1, Pallas kernels: none -> 55.3 us  [local(): pl.pallas_call(functools.partial(kernel, nz, nh, inner * nh), out_shape=j...]
    psum x1 -> x0, blocking collectives: 13.1 us -> none  [local(): square_sum = lax.psum(jnp.sum(mixed_out * mixed_out, axis=1), 'head')]
    dot_general x4 -> x0, matrix products: 7.6 us -> none  [the longest x1 5.01 us: local(): jnp.dot(placed, flat_weight, preferred_element_type=jnp.float32)]
    unnamed x12 -> x11, local copies, waits for them, and re-layouts: 10.7 us -> 4.56 us
  transfers between devices with their start and end apart: 1 -> 0, of which waited for: 1 -> 0; matrix products, arithmetic and copies ran while one was open for 0% -> 0% of each run, Pallas kernels for 0% -> 0%
where the time goes in v1:
time: 60.1 us; the launch traced here: 59.9 us
  Pallas kernels  55.3 us (92%)
  local copies, waits for them, and re-layouts  4.56 us (8%)
    pallas_call x1, Pallas kernels, local(): pl.pallas_call(functools.partial(kernel, nz, nh, inner * nh), out_shape=j...  55.3 us
    unnamed x11, local copies, waits for them, and re-layouts  4.56 us

profile of v1, /device:TPU:1, one launch (start us, length us, event | category | flops | bytes accessed | tf_op | source)
XLA Modules:
  0.0 59.9 jit_solution(12439739604237898017)
XLA Ops:
  0.0 0.0 copy-start
  0.0 1.1 %copy-done = bf16[128,3,1024]{2,0,1:T(8,128)(2,1)S(1)} copy-done((bf16[128,3,1024]{2,0,1:T(8,128)(2,1)S(1)}, bf16[128,3,1024]{2,0,1:T(8,128)(2,1)}, u32[]{:S(2)}) %copy-start) | copy-done | bytes 786456
  1.1 0.0 copy-start.1
  1.1 0.7 %copy-done.1 = bf16[4,1024]{1,0:T(4,128)(2,1)S(1)} copy-done((bf16[4,1024]{1,0:T(4,128)(2,1)S(1)}, bf16[4,1024]{1,0:T(4,128)(2,1)}, u32[]{:S(2)}) %copy-start.1) | copy-done | bytes 8216
  1.8 0.0 copy-start.2
  1.8 0.7 %copy-done.2 = f32[8,128]{1,0:T(8,128)S(1)} copy-done((f32[8,128]{1,0:T(8,128)S(1)}, f32[8,128]{1,0:T(8,128)}, u32[]{:S(2)}) %copy-start.2) | copy-done | bytes 4120
  2.5 0.0 copy-start.3
  2.5 0.7 %copy-done.3 = f32[1024]{0:T(1024)S(1)} copy-done((f32[1024]{0:T(1024)S(1)}, f32[1024]{0:T(1024)}, u32[]{:S(2)}) %copy-start.3) | copy-done | bytes 4120
  3.2 0.0 copy-start.4
  3.2 0.7 %copy-done.4 = s32[128]{0:T(128)S(1)} copy-done((s32[128]{0:T(128)S(1)}, s32[128]{0:T(128)}, u32[]{:S(2)}) %copy-start.4) | copy-done | bytes 536
  3.9 55.3 %lightning.1 = bf16[128,1024]{1,0:T(8,128)(2,1)S(1)} custom-call(bf16[3,128,1024]{2,1,0:T(8,128)(2,1)S(1)} %bitcast.4, bf16[4,1024]{1,0:T(4,128)(2,1)S(1)} %copy-done.1, bf16[3,1024,1024]{2,1,0:T(8,128)(2,1)} %bitcast.7, s32[1,128]{1,0:T(1,128)S(1)} %bitcast.6, f32[8,128]{1,0:T(8,128)S(1)} %copy-done.2, f32[1,1024]{1,0:T(1,128)S(1)} %bitcast.5), custom_call_target="tpu_custom_call" | custom-call | tf_op jit(solution)/shard_map/lightning/pallas_call | solution.py:352
  59.2 0.7 %copy.8 = bf16[128,1024]{1,0:T(8,128)(2,1)} copy(bf16[128,1024]{1,0:T(8,128)(2,1)S(1)} %lightning.1) | data formatting | bytes 524288
Async XLA Ops:
  0.0 1.1 %copy-start = (bf16[128,3,1024]{2,0,1:T(8,128)(2,1)S(1)}, bf16[128,3,1024]{2,0,1:T(8,128)(2,1)}, u32[]{:S(2)}) copy-start(bf16[128,3,1024]{2,0,1:T(8,128)(2,1)} %param.6) | copy-start | bytes 2359300
  1.1 0.7 %copy-start.1 = (bf16[4,1024]{1,0:T(4,128)(2,1)S(1)}, bf16[4,1024]{1,0:T(4,128)(2,1)}, u32[]{:S(2)}) copy-start(bf16[4,1024]{1,0:T(4,128)(2,1)} %feats.1) | copy-start | bytes 24580
  1.8 0.7 %copy-start.2 = (f32[8,128]{1,0:T(8,128)S(1)}, f32[8,128]{1,0:T(8,128)}, u32[]{:S(2)}) copy-start(f32[8,128]{1,0:T(8,128)} %log_decay.1) | copy-start | bytes 12292
  2.5 0.7 %copy-start.3 = (f32[1024]{0:T(1024)S(1)}, f32[1024]{0:T(1024)}, u32[]{:S(2)}) copy-start(f32[1024]{0:T(1024)} %param.11) | copy-start | bytes 12292
  3.2 0.7 %copy-start.4 = (s32[128]{0:T(128)S(1)}, s32[128]{0:T(128)}, u32[]{:S(2)}) copy-start(s32[128]{0:T(128)} %param.9) | copy-start | bytes 1540

commit v2 on v1

v2 whole, which is shorter than its diff:
```python
import functools

import jax
import jax.numpy as jnp
from jax import lax
from jax.experimental import pallas as pl
from jax.experimental.pallas import tpu as pltpu
from jax.sharding import PartitionSpec as P

MESH = pl.DeviceIdType.MESH
F32, BF16 = jnp.float32, jnp.bfloat16
NY = 8
FAR = -1e30
T = 128
TOT_Y, RAW_Y, FEAT_Y, TOT_Z, FEAT_X, FEAT_C, STATE_Z, BACK_Y, NORM, FEAT_Z, TAB_Z, BACK_Z, STATE_Y = range(13)
RINGS = {FEAT_Z: 16, TAB_Z: 32, BACK_Z: 48, STATE_Y: 64}
RECEIVES = 72


def halves(nz):
    half = nz // 2
    return (half, 4, 1) if half >= 6 else (half, half, 0)


def dot(a, b, dims=((1,), (0,))):
    return lax.dot_general(a, b, (dims, ((), ())), preferred_element_type=F32)


def lanes(h):
    start = h * T if isinstance(h, int) else pl.multiple_of(h * T, T)
    return pl.ds(start, T)


def kernel(
    nz, nh, heads_total,
    text_in, feats_in, w_in, vis_src_in, log_decay_in, gain_in, out,
    text, feats, w, vis_src, log_decay, gain, ybuf, fbuf, kv_sum, query_sum, kv_vis, query_all, s_out, s_in, e_out, e_in, pstate,
    t_out, t_in, r_out, r_in, raw, tot, tot_z, pre, tab_z, weight, decay, grown, mixed, part, norm,
    send, recv, load,
):
    nx = nh // 2
    vr = kv_vis.shape[1]
    yrows = 4 * NY
    half, owners, first = halves(nz)
    share = T // owners
    block_cols = fbuf.shape[3]
    inner = w.shape[2]
    me, hd = lax.axis_index("ctx"), lax.axis_index("head")
    z, y = me // NY, me % NY
    x, core = hd // 2, hd % 2
    base = z // half * half
    slot = z - base - first
    is_owner = (slot >= 0) & (slot < owners)
    block = core * nx + x

    def y_dev(to):
        return {"ctx": z * NY + to, "head": hd}

    def z_dev(to):
        return {"ctx": to * NY + y, "head": hd}

    def h_dev(to):
        return {"ctx": me, "head": to}

    leaving, arriving = [], []

    def put(src, dst, phase, device, receive=None):
        pltpu.make_async_remote_copy(
            src_ref=src, dst_ref=dst, send_sem=send.at[phase], recv_sem=recv.at[phase if receive is None else receive],
            device_id=device, device_id_type=MESH,
        ).start()

    def wait(ref, sem):
        pltpu.make_async_copy(ref, ref, sem).wait()

    def expect(phase, ref_out, ref_in):
        leaving.append(lambda: wait(ref_out, send.at[phase]))
        arriving.append((phase, lambda: wait(ref_in, recv.at[phase])))

    def arrived(phase):
        (entry,) = [e for e in arriving if e[0] == phase]
        arriving.remove(entry)
        entry[1]()

    def finish():
        for _, waiting in arriving + [(None, e) for e in leaving]:
            waiting()

    def y_peers():
        return [lax.rem(y + k, NY) for k in (4, 3, 5, 2, 6, 1, 7)]

    def z_peers():
        return [lax.rem(z + k, nz) for k in sorted(range(1, nz), key=lambda k: -min(k, nz - k))]

    def near(k, here, count):
        return lax.rem(here + (k % 2 * 2 - 1) * ((k + 1) // 2) + count, count)

    barrier = pltpu.get_barrier_semaphore()
    for to in y_peers():
        pl.semaphore_signal(barrier, inc=1, device_id=y_dev(to), device_id_type=MESH)
    for to in z_peers():
        pl.semaphore_signal(barrier, inc=1, device_id=z_dev(to), device_id_type=MESH)
    for k in range(1, nh):
        pl.semaphore_signal(barrier, inc=1, device_id=h_dev(lax.rem(hd + k, nh)), device_id_type=MESH)

    pairs = [(feats_in, feats), (log_decay_in, log_decay), (vis_src_in, vis_src), (text_in.at[2], text.at[2]),
             (text_in.at[1], text.at[1]), (text_in.at[0], text.at[0]), (gain_in, gain), (w_in, w)]
    loads = [pltpu.make_async_copy(src, dst, load.at[i]) for i, (src, dst) in enumerate(pairs)]
    for copy in loads:
        copy.start()

    loads[0].wait()
    quarters = [
        feats[:, pl.ds(pl.multiple_of((core * nx + c) * block_cols, T), block_cols)].astype(F32) for c in range(nx)
    ]
    ybuf[y] = jnp.concatenate(quarters, axis=0).astype(BF16)

    pl.semaphore_wait(barrier, NY - 1 + nz - 1 + nh - 1)
    for to in y_peers():
        put(ybuf.at[y], ybuf.at[y], FEAT_Y, y_dev(to))
    expect(FEAT_Y, ybuf.at[pl.ds(0, NY - 1)], ybuf.at[pl.ds(0, NY - 1)])

    loads[1].wait()
    lane = lax.broadcasted_iota(jnp.int32, (NY, T), 1)
    running = log_decay[...]
    step = 1
    while step < T:
        running = running + jnp.where(lane >= step, pltpu.roll(running, step, 1), 0.0)
        step *= 2

    def last_of(a):
        last = jnp.sum(jnp.where(lane == T - 1, a, 0.0), axis=1, keepdims=True)
        return jnp.broadcast_to(last, (NY, T))

    tot[y] = last_of(running)
    for to in y_peers():
        put(tot.at[y], tot.at[y], TOT_Y, y_dev(to))
    expect(TOT_Y, tot.at[pl.ds(0, NY - 1)], tot.at[pl.ds(0, NY - 1)])

    loads[2].wait()
    source_row = jnp.broadcast_to(vis_src[...], (T, T)).astype(F32)
    raw[y] = jnp.concatenate([running, source_row[:NY]], axis=0)
    source = source_row.T
    is_vis = source >= 0.0
    loads[3].wait()
    loads[4].wait()

    def head_state(h):
        row = jnp.broadcast_to(raw[y, pl.ds(h, 1), :], (T, T))
        last = jnp.broadcast_to(tot[y, pl.ds(h, 1), :], (T, T))
        tail = jnp.where(is_vis, 0.0, jnp.exp(last - row.T))
        value = text[2, :, lanes(h)].astype(F32) * tail
        high = value.astype(BF16)
        low = (value - high.astype(F32)).astype(BF16)
        both = dot(text[1, :, lanes(h)], jnp.concatenate([high, low], axis=1), ((0,), (0,)))
        s_out[h] = (both[:, :T] + both[:, T:]).astype(BF16)

    for h in range(NY):
        head_state(h)

    for p in range(owners):
        at = pl.ds(p * share, share)
        for to in y_peers():
            put(s_out.at[to, at], s_in.at[y, at], STATE_Y, y_dev(to), RINGS[STATE_Y] + p)
    leaving.append(lambda: wait(s_out.at[pl.ds(0, NY - 1)], send.at[STATE_Y]))
    for to in y_peers():
        put(raw.at[y], raw.at[y], RAW_Y, y_dev(to))
    expect(RAW_Y, raw.at[pl.ds(0, NY - 1)], raw.at[pl.ds(0, NY - 1)])
    s_in[y] = s_out[y]

    row_id = lax.broadcasted_iota(jnp.int32, (1, vr), 1).astype(F32)

    def one_hot(column):
        return jnp.concatenate(
            [jnp.where(column == row_id[:, j:j + T], 1.0, 0.0) for j in range(0, vr, T)], axis=1
        ).astype(BF16)

    pick = one_hot(source)

    arrived(FEAT_Y)
    rows = lax.broadcasted_iota(jnp.int32, (yrows, 4 * nx * NY), 0)
    folded = lax.broadcasted_iota(jnp.int32, (yrows, 4 * nx * NY), 1)
    wanted = lax.shift_right_logical(rows, 2) * (4 * nx) + x * 4 + (rows & 3)
    unfold = jnp.where(wanted == folded, 1.0, 0.0).astype(BF16)
    fbuf[block, z] = dot(unfold, ybuf[...].reshape(4 * nx * NY, block_cols)).astype(BF16)
    for to in z_peers():
        put(fbuf.at[block, z], fbuf.at[block, z], FEAT_Z, z_dev(to), RINGS[FEAT_Z] + z)
    leaving.append(lambda: wait(fbuf.at[0, pl.ds(0, nz - 1)], send.at[FEAT_Z]))

    arrived(TOT_Y)
    before = jnp.zeros((NY, T), F32)
    for k in range(NY):
        pre[k] = before
        before = before + tot[k]
    tot_z[z] = before
    for to in z_peers():
        put(tot_z.at[z], tot_z.at[z], TOT_Z, z_dev(to))
    expect(TOT_Z, tot_z.at[pl.ds(0, nz - 1)], tot_z.at[pl.ds(0, nz - 1)])

    causal = lax.broadcasted_iota(jnp.int32, (T, T), 0) >= lax.broadcasted_iota(jnp.int32, (T, T), 1)

    def head_decay(h):
        row = jnp.broadcast_to(raw[y, pl.ds(h, 1), :], (T, T))
        col = row.T
        grown[h] = jnp.exp(col)
        decay[h] = jnp.where(causal, jnp.exp(jnp.where(causal, col - row, 0.0)), 0.0)

    for h in range(NY):
        head_decay(h)

    def forward(k, _):
        piece = fbuf.at[block, near(k, z, nz)]

        @pl.when(k > 0)
        def _():
            wait(piece, recv.at[RINGS[FEAT_Z] + near(k, z, nz)])

        for j in range(1, nx):
            put(piece, piece, FEAT_X, h_dev(lax.rem(x + j, nx) * 2 + core))
        put(piece, piece, FEAT_C, h_dev(x * 2 + 1 - core))
        return 0

    early = nz // 2 + 1
    for p in range(owners):
        at = pl.ds(p * share, share)
        wait(s_in.at[pl.ds(0, NY - 1), at], recv.at[RINGS[STATE_Y] + p])
        state = jnp.zeros((share, T), F32)
        for k in range(NY):
            pstate[k, at] = state
            state = state * jnp.exp(tot[k, pl.ds(y, 1), :]) + s_in[k, at].astype(F32)
        t_out[p] = state
        for begin, last in ((0, half - 2), (half, nz - 2)):
            owner = begin + first + p

            @pl.when((z != owner) & (z <= last))
            def _():
                put(t_out.at[p], t_in.at[z], STATE_Z, z_dev(owner))

    def state_z_left():
        for k in range(nz):
            targets = [
                begin + first + p for begin, last in ((0, half - 2), (half, nz - 2)) if k <= last for p in range(owners)
                if begin + first + p != k
            ]

            @pl.when(z == k)
            def _():
                if targets:
                    wait(t_in.at[pl.ds(0, len(targets))], send.at[STATE_Z])

    def state_z_here():
        for k in range(nz):
            begin = k // half * half
            sources = [i for i in range(nz) if i <= begin + half - 2 and i != k]

            @pl.when((z == k) & is_owner)
            def _():
                if sources:
                    wait(t_in.at[pl.ds(0, len(sources))], recv.at[STATE_Z])

    leaving.append(state_z_left)
    arriving.append((STATE_Z, state_z_here))

    lax.fori_loop(0, early, forward, 0)

    arrived(RAW_Y)
    to_end, to_own = [None] * NY, [None] * NY
    after, after_own = jnp.zeros((NY, T), F32), jnp.zeros((NY, T), F32)
    for k in reversed(range(NY)):
        rest = tot[k] - raw[k, :NY]
        mine = jnp.full((NY, T), k, jnp.int32) < y
        to_end[k] = rest + after
        to_own[k] = jnp.where(mine, rest + after_own, 0.0)
        after = after + tot[k]
        after_own = after_own + jnp.where(mine, tot[k], 0.0)
    pieces = []
    for group in (to_end, to_own):
        logs = jnp.concatenate(group, axis=1)
        high = logs.astype(BF16).astype(F32)
        mid = (logs - high).astype(BF16).astype(F32)
        pieces += [high, mid, logs - high - mid]
    reach = lax.broadcasted_iota(jnp.int32, (NY, NY * T), 1) < y * T
    pieces += [jnp.ones((NY, NY * T), F32), jnp.where(reach, 1.0, 0.0)]
    hot = jnp.concatenate(
        [one_hot(jnp.broadcast_to(raw[k, pl.ds(NY, 1), :], (T, T)).T) for k in range(NY)], axis=0
    )
    table = dot(jnp.concatenate(pieces, axis=0).astype(BF16), hot)
    table = [table[i * NY:(i + 1) * NY] for i in range(8)]
    row_tab = jnp.where(table[6] > 0.5, table[0] + table[1] + table[2], FAR)
    own_tab = jnp.where(table[7] > 0.5, table[3] + table[4] + table[5], FAR)
    tab_z[z] = row_tab
    for to in z_peers():
        @pl.when(to > z)
        def _():
            put(tab_z.at[z], tab_z.at[z], TAB_Z, z_dev(to), RINGS[TAB_Z] + z)

    def tab_z_left():
        for k in range(nz):
            @pl.when(z == k)
            def _():
                if k < nz - 1:
                    wait(tab_z.at[pl.ds(0, nz - 1 - k)], send.at[TAB_Z])

    leaving.append(tab_z_left)

    def wide(a):
        return jnp.concatenate([a] * (vr // T), axis=1)

    lax.fori_loop(early, nz, forward, 0)
    slabs = fbuf.at[pl.ds(0, nx - 1)]
    expect(FEAT_X, slabs, slabs)

    arrived(TOT_Z)
    arrived(STATE_Z)

    @pl.when(is_owner)
    def _():
        t_in[z] = t_out[slot]

    for begin in (0, half):
        @pl.when(is_owner & (base == begin))
        def _():
            carry = jnp.zeros((share, T), F32)
            for k in range(begin + half):
                if k >= begin:
                    r_out[k] = carry
                if k < begin + half - 1:
                    carry = carry * jnp.exp(tot_z[k, pl.ds(y, 1), :]) + t_in[k]
            for k in range(max(begin, 1), begin + half):
                @pl.when(z != k)
                def _():
                    put(r_out.at[k], r_in.at[slot], BACK_Z, z_dev(k), RINGS[BACK_Z] + slot)

    @pl.when(is_owner)
    def _():
        r_in[slot] = r_out[z]

    @pl.when(z == 0)
    def _():
        r_in[...] = jnp.zeros_like(r_in)

    def back_z_left():
        for k in range(nz):
            begin = k // half * half
            targets = [i for i in range(max(begin, 1), begin + half) if i != k]

            @pl.when((z == k) & is_owner)
            def _():
                if targets:
                    wait(r_out.at[pl.ds(0, len(targets))], send.at[BACK_Z])

    leaving.append(back_z_left)

    arrived(FEAT_X)
    for j in range(1, nx):
        slab = fbuf.at[core * nx + lax.rem(x + j, nx)]
        put(slab, slab, FEAT_C, h_dev(x * 2 + 1 - core))
    expect(FEAT_C, fbuf.at[pl.ds(0, nx)], fbuf.at[pl.ds(0, nx)])

    for copy in loads[5:]:
        copy.wait()
    chunk = 256

    def feature_half(side):
        columns = [fbuf[side * nx + j].reshape(vr, block_cols) for j in range(nx)]
        size = nx * block_cols
        return jnp.concatenate(columns, axis=1), pl.ds(pl.multiple_of(side * size, size), size)

    near_side, near_rows = feature_half(core)
    for m in range(2):
        for start in range(0, inner, chunk):
            cols = pl.ds(start, chunk)
            kv_sum[m, :, cols] = dot(near_side, w[m + 1, near_rows, cols])
    placed = dot(pick, near_side).astype(BF16)
    for start in range(0, inner, chunk):
        cols = pl.ds(start, chunk)
        query_sum[:, cols] = dot(placed, w[0, near_rows, cols])

    def enter(owner, _):
        @pl.when((owner != slot) & (z > 0))
        def _():
            wait(r_in.at[owner], recv.at[RINGS[BACK_Z] + owner])

        at = pl.ds(pl.multiple_of(owner * share, share), share)
        entering = r_in[owner]
        for to in y_peers():
            e_out[to, at] = (pstate[to, at] + entering * jnp.exp(pre[to, pl.ds(y, 1), :])).astype(BF16)
            put(e_out.at[to, at], e_in.at[y, at], BACK_Y, y_dev(to))
        e_in[y, at] = (pstate[y, at] + entering * jnp.exp(pre[y, pl.ds(y, 1), :])).astype(BF16)
        return 0

    lax.fori_loop(0, owners, enter, 0)
    expect(BACK_Y, e_out.at[pl.ds(0, NY - 1)], e_in.at[pl.ds(0, NY - 1)])

    weight[...] = jnp.full((NY, vr), FAR, F32)
    for k in range(nz - 1):
        @pl.when(k < z)
        def _():
            wait(tab_z.at[k], recv.at[RINGS[TAB_Z] + k])
            weight[...] = jnp.maximum(weight[...] + wide(tot_z[k]), tab_z[k])

    weight[...] = jnp.exp(jnp.maximum(weight[...] + wide(pre[y]), own_tab))

    arrived(FEAT_C)
    far_side, far_rows = feature_half(1 - core)
    for m in range(2):
        for start in range(0, inner, chunk):
            cols = pl.ds(start, chunk)
            kv_vis[m, :, cols] = (kv_sum[m, :, cols] + dot(far_side, w[m + 1, far_rows, cols])).astype(BF16)
    placed = dot(pick, far_side).astype(BF16)
    for start in range(0, inner, chunk):
        cols = pl.ds(start, chunk)
        query = (query_sum[:, cols] + dot(placed, w[0, far_rows, cols])).astype(BF16).astype(F32)
        mask = jnp.concatenate([is_vis] * (chunk // T), axis=1)
        query_all[:, cols] = jnp.where(mask, query, text[0, :, cols].astype(F32)).astype(BF16)

    def head_within(h):
        at = lanes(h)
        query = query_all[:, at]
        key, value = [
            jnp.where(is_vis, dot(pick, kv_vis[m, :, at]), text[m + 1, :, at].astype(F32)).astype(BF16) for m in range(2)
        ]
        weights = (dot(query, key, ((1,), (1,))) * decay[h]).astype(BF16)
        mixed[:, at] = dot(weights, value)
        visual = dot(query, kv_vis[0, :, at], ((1,), (1,))) * weight[pl.ds(h, 1), :]
        part[:, at] = dot(visual.astype(BF16), kv_vis[1, :, at])

    for h in range(NY):
        head_within(h)

    arrived(BACK_Y)
    squares = jnp.zeros((T, T), F32)
    for h in range(NY):
        at = lanes(h)
        result = mixed[:, at] + grown[h] * (dot(query_all[:, at], e_in[h]) + part[:, at])
        mixed[:, at] = result
        squares = squares + result * result

    norm[hd] = jnp.broadcast_to(jnp.sum(squares.T, axis=0, keepdims=True), (8, T))
    for k in range(1, nh):
        put(norm.at[hd], norm.at[hd], NORM, h_dev(lax.rem(hd + k, nh)))
    expect(NORM, norm.at[pl.ds(0, nh - 1)], norm.at[pl.ds(0, nh - 1)])
    arrived(NORM)
    square_sum = norm[0]
    for k in range(1, nh):
        square_sum = square_sum + norm[k]
    inverse = lax.rsqrt(square_sum * (1.0 / heads_total) + 1e-05)
    scale = jnp.broadcast_to(inverse[:1], (T, T)).T
    for h in range(NY):
        at = lanes(h)
        out[:, at] = (mixed[:, at] * scale * gain[:, at]).astype(BF16)

    finish()


def hbm(a):
    return pltpu.with_memory_space_constraint(a, pltpu.HBM)


def local(nz, nh, text_qkv, vis_feats, w_visual, vis_src, log_decay, norm_gain):
    row_count, _, inner = text_qkv.shape
    width = vis_feats.shape[1]
    vr = vis_feats.shape[0] * NY * nz
    _, owners, _ = halves(nz)
    share = T // owners
    vmem = pl.BlockSpec(memory_space=pltpu.VMEM)
    anywhere = pl.BlockSpec(memory_space=pltpu.HBM)
    scratch = [
        pltpu.VMEM((3, row_count, inner), BF16),
        pltpu.VMEM(vis_feats.shape, BF16),
        pltpu.VMEM((3, width, inner), BF16),
        pltpu.VMEM((1, row_count), jnp.int32),
        pltpu.VMEM(log_decay.shape, F32),
        pltpu.VMEM((1, inner), F32),
        pltpu.VMEM((NY, 4 * (nh // 2), width // nh), BF16),
        pltpu.VMEM((nh, nz, 4 * NY, width // nh), BF16),
        pltpu.VMEM((2, vr, inner), F32),
        pltpu.VMEM((row_count, inner), F32),
        pltpu.VMEM((2, vr, inner), BF16),
        pltpu.VMEM((row_count, inner), BF16),
        pltpu.VMEM((NY, T, T), BF16),
        pltpu.VMEM((NY, T, T), BF16),
        pltpu.VMEM((NY, T, T), BF16),
        pltpu.VMEM((NY, T, T), BF16),
        pltpu.VMEM((NY, T, T), F32),
        pltpu.VMEM((owners, share, T), F32),
        pltpu.VMEM((nz, share, T), F32),
        pltpu.VMEM((nz, share, T), F32),
        pltpu.VMEM((owners, share, T), F32),
        pltpu.VMEM((NY, 2 * NY, T), F32),
        pltpu.VMEM((NY, NY, T), F32),
        pltpu.VMEM((nz, NY, T), F32),
        pltpu.VMEM((NY, NY, T), F32),
        pltpu.VMEM((nz, NY, vr), F32),
        pltpu.VMEM((NY, vr), F32),
        pltpu.VMEM((NY, T, T), F32),
        pltpu.VMEM((NY, T, T), F32),
        pltpu.VMEM((row_count, inner), F32),
        pltpu.VMEM((row_count, inner), F32),
        pltpu.VMEM((nh, 8, T), F32),
        pltpu.SemaphoreType.DMA((13,)),
        pltpu.SemaphoreType.DMA((RECEIVES,)),
        pltpu.SemaphoreType.DMA((8,)),
    ]
    return pl.pallas_call(
        functools.partial(kernel, nz, nh, inner * nh),
        out_shape=jax.ShapeDtypeStruct((row_count, inner), BF16),
        in_specs=[anywhere] * 6,
        out_specs=vmem,
        scratch_shapes=scratch,
        compiler_params=pltpu.CompilerParams(
            collective_id=0, has_side_effects=True, vmem_limit_bytes=48 * 1024 * 1024
        ),
        name="lightning",
    )(
        hbm(text_qkv.transpose(1, 0, 2)),
        hbm(vis_feats),
        hbm(w_visual.transpose(1, 0, 2)),
        hbm(vis_src.reshape(1, row_count)),
        hbm(log_decay),
        hbm(norm_gain.reshape(1, inner)),
    )


def solution(mesh):
    placed = (
        P("ctx", None, "head"),
        P("ctx", None),
        P(None, None, "head"),
        P("ctx"),
        P("head", "ctx"),
        P("head"),
    )
    nz, nh = mesh.shape["ctx"] // NY, mesh.shape["head"]
    return jax.shard_map(
        functools.partial(local, nz, nh), mesh=mesh, in_specs=placed, out_specs=P("ctx", "head"), check_vma=False
    )
```

time: 60.1 us -> 49.5 us (0.82)
  Pallas kernels: 55.3 us -> 48.6 us
  local copies, waits for them, and re-layouts: 4.56 us -> 0.71 us
    pallas_call x1, Pallas kernels: 55.3 us -> 48.6 us  [local(): pl.pallas_call(functools.partial(kernel, nz, nh, inner * nh), out_shape=j...]
    unnamed x11 -> x1, local copies, waits for them, and re-layouts: 4.56 us -> 0.71 us
where the time goes in v2:
time: 49.5 us; the launch traced here: 49.3 us
  Pallas kernels  48.6 us (98%)
  local copies, waits for them, and re-layouts  0.71 us (1%)
    pallas_call x1, Pallas kernels, local(): pl.pallas_call(functools.partial(kernel, nz, nh, inner * nh), out_shape=j...  48.6 us

profile of v2, /device:TPU:1, one launch (start us, length us, event | category | flops | bytes accessed | tf_op | source)
XLA Modules:
  0.0 49.3 jit_solution(9951435132320566610)
XLA Ops:
  0.0 48.6 %lightning.1 = bf16[128,1024]{1,0:T(8,128)(2,1)S(1)} custom-call(bf16[3,128,1024]{2,1,0:T(8,128)(2,1)} %bitcast.5, bf16[4,1024]{1,0:T(4,128)(2,1)} %feats_in.1, bf16[3,1024,1024]{2,1,0:T(8,128)(2,1)} %bitcast.4, s32[1,128]{1,0:T(1,128)} %bitcast.7, f32[8,128]{1,0:T(8,128)} %log_decay_in.1, f32[1,1024]{1,0:T(1,128)} %bitcast.6), custom_call_target="tpu_custom_call" | custom-call | tf_op jit(solution)/shard_map/lightning/pallas_call | solution.py:505
  48.6 0.7 %copy.8 = bf16[128,1024]{1,0:T(8,128)(2,1)} copy(bf16[128,1024]{1,0:T(8,128)(2,1)S(1)} %lightning.1) | data formatting | bytes 524288

commit v3 on v2

--- a/solution.py
+++ b/solution.py
@@ -34,12 +34,12 @@
 def kernel(
     nz, nh, heads_total,
     text_in, feats_in, w_in, vis_src_in, log_decay_in, gain_in, out,
-    text, feats, w, vis_src, log_decay, gain, ybuf, fbuf, kv_sum, query_sum, kv_vis, query_all, s_out, s_in, e_out, e_in, pstate,
-    t_out, t_in, r_out, r_in, raw, tot, tot_z, pre, tab_z, weight, decay, grown, mixed, part, norm,
+    text, feats, w, vis_src, log_decay, gain, ybuf, fbuf, kv_sum, query_sum, kv_all, query_all, s_out, s_in, e_out, e_in, pstate,
+    t_out, t_in, r_out, r_in, raw, tot, tot_z, pre, tab_z, weight, factor, grown, mixed, norm,
     send, recv, load,
 ):
     nx = nh // 2
-    vr = kv_vis.shape[1]
+    vr = kv_sum.shape[1]
     yrows = 4 * NY
     half, owners, first = halves(nz)
     share = T // owners
@@ -96,10 +96,10 @@
         return lax.rem(here + (k % 2 * 2 - 1) * ((k + 1) // 2) + count, count)
 
     barrier = pltpu.get_barrier_semaphore()
+    for to in z_peers():
+        pl.semaphore_signal(barrier, inc=1, device_id=z_dev(to), device_id_type=MESH)
     for to in y_peers():
         pl.semaphore_signal(barrier, inc=1, device_id=y_dev(to), device_id_type=MESH)
-    for to in z_peers():
-        pl.semaphore_signal(barrier, inc=1, device_id=z_dev(to), device_id_type=MESH)
     for k in range(1, nh):
         pl.semaphore_signal(barrier, inc=1, device_id=h_dev(lax.rem(hd + k, nh)), device_id_type=MESH)
 
@@ -197,28 +197,30 @@
         put(tot_z.at[z], tot_z.at[z], TOT_Z, z_dev(to))
     expect(TOT_Z, tot_z.at[pl.ds(0, nz - 1)], tot_z.at[pl.ds(0, nz - 1)])
 
+    def forward(k, _):
+        piece = fbuf.at[block, near(k, z, nz)]
+
+        @pl.when(k > 0)
+        def _():
+            wait(piece, recv.at[RINGS[FEAT_Z] + near(k, z, nz)])
+
+        for j in range(1, nx):
+            put(piece, piece, FEAT_X, h_dev(lax.rem(x + j, nx) * 2 + core))
+        put(piece, piece, FEAT_C, h_dev(x * 2 + 1 - core))
+        return 0
+
+    lax.fori_loop(0, 1, forward, 0)
+
     causal = lax.broadcasted_iota(jnp.int32, (T, T), 0) >= lax.broadcasted_iota(jnp.int32, (T, T), 1)
 
     def head_decay(h):
         row = jnp.broadcast_to(raw[y, pl.ds(h, 1), :], (T, T))
         col = row.T
         grown[h] = jnp.exp(col)
-        decay[h] = jnp.where(causal, jnp.exp(jnp.where(causal, col - row, 0.0)), 0.0)
+        factor[h, :, vr:] = jnp.where(causal, jnp.exp(jnp.where(causal, col - row, 0.0)), 0.0)
 
     for h in range(NY):
         head_decay(h)
-
-    def forward(k, _):
-        piece = fbuf.at[block, near(k, z, nz)]
-
-        @pl.when(k > 0)
-        def _():
-            wait(piece, recv.at[RINGS[FEAT_Z] + near(k, z, nz)])
-
-        for j in range(1, nx):
-            put(piece, piece, FEAT_X, h_dev(lax.rem(x + j, nx) * 2 + core))
-        put(piece, piece, FEAT_C, h_dev(x * 2 + 1 - core))
-        return 0
 
     early = nz // 2 + 1
     for p in range(owners):
@@ -229,12 +231,35 @@
             pstate[k, at] = state
             state = state * jnp.exp(tot[k, pl.ds(y, 1), :]) + s_in[k, at].astype(F32)
         t_out[p] = state
+
+        @pl.when(z == 0)
+        def _():
+            put(t_out.at[p], r_in.at[p], BACK_Z, z_dev(1), RINGS[BACK_Z] + p)
+
         for begin, last in ((0, half - 2), (half, nz - 2)):
             owner = begin + first + p
 
             @pl.when((z != owner) & (z <= last))
             def _():
                 put(t_out.at[p], t_in.at[z], STATE_Z, z_dev(owner))
+
+    def enter(owner, _):
+        @pl.when((z == 1) | ((z > 1) & (owner != slot)))
+        def _():
+            wait(r_in.at[owner], recv.at[RINGS[BACK_Z] + owner])
+
+        at = pl.ds(pl.multiple_of(owner * share, share), share)
+        entering = r_in[owner]
+        for to in y_peers():
+            e_out[to, at] = (pstate[to, at] + entering * jnp.exp(pre[to, pl.ds(y, 1), :])).astype(BF16)
+            put(e_out.at[to, at], e_in.at[y, at], BACK_Y, y_dev(to))
+        e_in[y, at] = (pstate[y, at] + entering * jnp.exp(pre[y, pl.ds(y, 1), :])).astype(BF16)
+        return 0
+
+    @pl.when(z == 0)
+    def _():
+        r_in[...] = jnp.zeros_like(r_in)
+        lax.fori_loop(0, owners, enter, 0)
 
     def state_z_left():
         for k in range(nz):
@@ -261,7 +286,7 @@
     leaving.append(state_z_left)
     arriving.append((STATE_Z, state_z_here))
 
-    lax.fori_loop(0, early, forward, 0)
+    lax.fori_loop(1, early, forward, 0)
 
     arrived(RAW_Y)
     to_end, to_own = [None] * NY, [None] * NY
@@ -326,30 +351,34 @@
                     r_out[k] = carry
                 if k < begin + half - 1:
                     carry = carry * jnp.exp(tot_z[k, pl.ds(y, 1), :]) + t_in[k]
-            for k in range(max(begin, 1), begin + half):
+            for k in range(max(begin, 2), begin + half):
                 @pl.when(z != k)
                 def _():
                     put(r_out.at[k], r_in.at[slot], BACK_Z, z_dev(k), RINGS[BACK_Z] + slot)
 
-    @pl.when(is_owner)
+    @pl.when(is_owner & (z > 1))
     def _():
         r_in[slot] = r_out[z]
-
-    @pl.when(z == 0)
-    def _():
-        r_in[...] = jnp.zeros_like(r_in)
 
     def back_z_left():
         for k in range(nz):
             begin = k // half * half
-            targets = [i for i in range(max(begin, 1), begin + half) if i != k]
+            targets = [i for i in range(max(begin, 2), begin + half) if i != k]
 
             @pl.when((z == k) & is_owner)
             def _():
                 if targets:
                     wait(r_out.at[pl.ds(0, len(targets))], send.at[BACK_Z])
 
+        @pl.when(z == 0)
+        def _():
+            wait(t_out, send.at[BACK_Z])
+
     leaving.append(back_z_left)
+
+    @pl.when(z == 1)
+    def _():
+        lax.fori_loop(0, owners, enter, 0)
 
     arrived(FEAT_X)
     for j in range(1, nx):
@@ -376,20 +405,10 @@
         cols = pl.ds(start, chunk)
         query_sum[:, cols] = dot(placed, w[0, near_rows, cols])
 
-    def enter(owner, _):
-        @pl.when((owner != slot) & (z > 0))
-        def _():
-            wait(r_in.at[owner], recv.at[RINGS[BACK_Z] + owner])
-
-        at = pl.ds(pl.multiple_of(owner * share, share), share)
-        entering = r_in[owner]
-        for to in y_peers():
-            e_out[to, at] = (pstate[to, at] + entering * jnp.exp(pre[to, pl.ds(y, 1), :])).astype(BF16)
-            put(e_out.at[to, at], e_in.at[y, at], BACK_Y, y_dev(to))
-        e_in[y, at] = (pstate[y, at] + entering * jnp.exp(pre[y, pl.ds(y, 1), :])).astype(BF16)
-        return 0
-
-    lax.fori_loop(0, owners, enter, 0)
+    @pl.when(z > 1)
+    def _():
+        lax.fori_loop(0, owners, enter, 0)
+
     expect(BACK_Y, e_out.at[pl.ds(0, NY - 1)], e_in.at[pl.ds(0, NY - 1)])
 
     weight[...] = jnp.full((NY, vr), FAR, F32)
@@ -400,30 +419,30 @@
             weight[...] = jnp.maximum(weight[...] + wide(tot_z[k]), tab_z[k])
 
     weight[...] = jnp.exp(jnp.maximum(weight[...] + wide(pre[y]), own_tab))
+    for h in range(NY):
+        factor[h, :, :vr] = wide(grown[h]) * weight[pl.ds(h, 1), :]
 
     arrived(FEAT_C)
     far_side, far_rows = feature_half(1 - core)
+    mask = jnp.concatenate([is_vis] * (chunk // T), axis=1)
     for m in range(2):
         for start in range(0, inner, chunk):
             cols = pl.ds(start, chunk)
-            kv_vis[m, :, cols] = (kv_sum[m, :, cols] + dot(far_side, w[m + 1, far_rows, cols])).astype(BF16)
+            visual = (kv_sum[m, :, cols] + dot(far_side, w[m + 1, far_rows, cols])).astype(BF16)
+            kv_all[m, :vr, cols] = visual
+            own = jnp.where(mask, dot(pick, visual), text[m + 1, :, cols].astype(F32))
+            kv_all[m, vr:, cols] = own.astype(BF16)
     placed = dot(pick, far_side).astype(BF16)
     for start in range(0, inner, chunk):
         cols = pl.ds(start, chunk)
         query = (query_sum[:, cols] + dot(placed, w[0, far_rows, cols])).astype(BF16).astype(F32)
-        mask = jnp.concatenate([is_vis] * (chunk // T), axis=1)
         query_all[:, cols] = jnp.where(mask, query, text[0, :, cols].astype(F32)).astype(BF16)
 
     def head_within(h):
         at = lanes(h)
         query = query_all[:, at]
-        key, value = [
-            jnp.where(is_vis, dot(pick, kv_vis[m, :, at]), text[m + 1, :, at].astype(F32)).astype(BF16) for m in range(2)
-        ]
-        weights = (dot(query, key, ((1,), (1,))) * decay[h]).astype(BF16)
-        mixed[:, at] = dot(weights, value)
-        visual = dot(query, kv_vis[0, :, at], ((1,), (1,))) * weight[pl.ds(h, 1), :]
-        part[:, at] = dot(visual.astype(BF16), kv_vis[1, :, at])
+        weights = dot(query, kv_all[0, :, at], ((1,), (1,))) * factor[h]
+        mixed[:, at] = dot(weights.astype(BF16), kv_all[1, :, at])
 
     for h in range(NY):
         head_within(h)
@@ -432,7 +451,7 @@
     squares = jnp.zeros((T, T), F32)
     for h in range(NY):
         at = lanes(h)
-        result = mixed[:, at] + grown[h] * (dot(query_all[:, at], e_in[h]) + part[:, at])
+        result = mixed[:, at] + grown[h] * dot(query_all[:, at], e_in[h])
         mixed[:, at] = result
         squares = squares + result * result
 
@@ -476,7 +495,7 @@
         pltpu.VMEM((nh, nz, 4 * NY, width // nh), BF16),
         pltpu.VMEM((2, vr, inner), F32),
         pltpu.VMEM((row_count, inner), F32),
-        pltpu.VMEM((2, vr, inner), BF16),
+        pltpu.VMEM((2, vr + row_count, inner), BF16),
         pltpu.VMEM((row_count, inner), BF16),
         pltpu.VMEM((NY, T, T), BF16),
         pltpu.VMEM((NY, T, T), BF16),
@@ -493,9 +512,8 @@
         pltpu.VMEM((NY, NY, T), F32),
         pltpu.VMEM((nz, NY, vr), F32),
         pltpu.VMEM((NY, vr), F32),
+        pltpu.VMEM((NY, T, vr + T), F32),
         pltpu.VMEM((NY, T, T), F32),
-        pltpu.VMEM((NY, T, T), F32),
-        pltpu.VMEM((row_count, inner), F32),
         pltpu.VMEM((row_count, inner), F32),
         pltpu.VMEM((nh, 8, T), F32),
         pltpu.SemaphoreType.DMA((13,)),

time: 49.5 us -> 47.5 us (0.960)
  Pallas kernels: 48.6 us -> 46.6 us
    pallas_call x1, Pallas kernels: 48.6 us -> 46.6 us  [local(): pl.pallas_call(functools.partial(kernel, nz, nh, inner * nh), out_shape=j...]
where the time goes in v3:
time: 47.5 us; the launch traced here: 47.3 us
  Pallas kernels  46.6 us (98%)
  local copies, waits for them, and re-layouts  0.71 us (1%)
    pallas_call x1, Pallas kernels, local(): pl.pallas_call(functools.partial(kernel, nz, nh, inner * nh), out_shape=j...  46.6 us

profile of v3, /device:TPU:1, one launch (start us, length us, event | category | flops | bytes accessed | tf_op | source)
XLA Modules:
  0.0 47.3 jit_solution(16245253100685216419)
XLA Ops:
  0.0 46.6 %lightning.1 = bf16[128,1024]{1,0:T(8,128)(2,1)S(1)} custom-call(bf16[3,128,1024]{2,1,0:T(8,128)(2,1)} %bitcast.5, bf16[4,1024]{1,0:T(4,128)(2,1)} %feats_in.1, bf16[3,1024,1024]{2,1,0:T(8,128)(2,1)} %bitcast.4, s32[1,128]{1,0:T(1,128)} %bitcast.7, f32[8,128]{1,0:T(8,128)} %log_decay_in.1, f32[1,1024]{1,0:T(1,128)} %bitcast.6), custom_call_target="tpu_custom_call" | custom-call | tf_op jit(solution)/shard_map/lightning/pallas_call | solution.py:523
  46.6 0.7 %copy.8 = bf16[128,1024]{1,0:T(8,128)(2,1)} copy(bf16[128,1024]{1,0:T(8,128)(2,1)S(1)} %lightning.1) | data formatting | bytes 524288

commit v4 on v3

--- a/solution.py
+++ b/solution.py
@@ -13,8 +13,8 @@
 FAR = -1e30
 T = 128
 TOT_Y, RAW_Y, FEAT_Y, TOT_Z, FEAT_X, FEAT_C, STATE_Z, BACK_Y, NORM, FEAT_Z, TAB_Z, BACK_Z, STATE_Y = range(13)
-RINGS = {FEAT_Z: 16, TAB_Z: 32, BACK_Z: 48, STATE_Y: 64}
-RECEIVES = 72
+RINGS = {FEAT_X: 72, FEAT_Z: 16, TAB_Z: 32, BACK_Z: 48, STATE_Y: 64}
+RECEIVES = 80
 
 
 def halves(nz):
@@ -83,7 +83,7 @@
         entry[1]()
 
     def finish():
-        for _, waiting in arriving + [(None, e) for e in leaving]:
+        for waiting in leaving + [e for _, e in arriving]:
             waiting()
 
     def y_peers():
@@ -115,11 +115,6 @@
     ]
     ybuf[y] = jnp.concatenate(quarters, axis=0).astype(BF16)
 
-    pl.semaphore_wait(barrier, NY - 1 + nz - 1 + nh - 1)
-    for to in y_peers():
-        put(ybuf.at[y], ybuf.at[y], FEAT_Y, y_dev(to))
-    expect(FEAT_Y, ybuf.at[pl.ds(0, NY - 1)], ybuf.at[pl.ds(0, NY - 1)])
-
     loads[1].wait()
     lane = lax.broadcasted_iota(jnp.int32, (NY, T), 1)
     running = log_decay[...]
@@ -133,9 +128,6 @@
         return jnp.broadcast_to(last, (NY, T))
 
     tot[y] = last_of(running)
-    for to in y_peers():
-        put(tot.at[y], tot.at[y], TOT_Y, y_dev(to))
-    expect(TOT_Y, tot.at[pl.ds(0, NY - 1)], tot.at[pl.ds(0, NY - 1)])
 
     loads[2].wait()
     source_row = jnp.broadcast_to(vis_src[...], (T, T)).astype(F32)
@@ -158,6 +150,13 @@
     for h in range(NY):
         head_state(h)
 
+    pl.semaphore_wait(barrier, NY - 1 + nz - 1 + nh - 1)
+    for to in y_peers():
+        put(ybuf.at[y], ybuf.at[y], FEAT_Y, y_dev(to))
+    expect(FEAT_Y, ybuf.at[pl.ds(0, NY - 1)], ybuf.at[pl.ds(0, NY - 1)])
+    for to in y_peers():
+        put(tot.at[y], tot.at[y], TOT_Y, y_dev(to))
+    expect(TOT_Y, tot.at[pl.ds(0, NY - 1)], tot.at[pl.ds(0, NY - 1)])
     for p in range(owners):
         at = pl.ds(p * share, share)
         for to in y_peers():
@@ -205,7 +204,7 @@
             wait(piece, recv.at[RINGS[FEAT_Z] + near(k, z, nz)])
 
         for j in range(1, nx):
-            put(piece, piece, FEAT_X, h_dev(lax.rem(x + j, nx) * 2 + core))
+            put(piece, piece, FEAT_X, h_dev(lax.rem(x + j, nx) * 2 + core), RINGS[FEAT_X] + x)
         put(piece, piece, FEAT_C, h_dev(x * 2 + 1 - core))
         return 0
 
@@ -314,11 +313,6 @@
     row_tab = jnp.where(table[6] > 0.5, table[0] + table[1] + table[2], FAR)
     own_tab = jnp.where(table[7] > 0.5, table[3] + table[4] + table[5], FAR)
     tab_z[z] = row_tab
-    for to in z_peers():
-        @pl.when(to > z)
-        def _():
-            put(tab_z.at[z], tab_z.at[z], TAB_Z, z_dev(to), RINGS[TAB_Z] + z)
-
     def tab_z_left():
         for k in range(nz):
             @pl.when(z == k)
@@ -332,8 +326,7 @@
         return jnp.concatenate([a] * (vr // T), axis=1)
 
     lax.fori_loop(early, nz, forward, 0)
-    slabs = fbuf.at[pl.ds(0, nx - 1)]
-    expect(FEAT_X, slabs, slabs)
+    leaving.append(lambda: wait(fbuf.at[pl.ds(0, nx - 1)], send.at[FEAT_X]))
 
     arrived(TOT_Z)
     arrived(STATE_Z)
@@ -376,13 +369,18 @@
 
     leaving.append(back_z_left)
 
+    for to in z_peers():
+        @pl.when(to > z)
+        def _():
+            put(tab_z.at[z], tab_z.at[z], TAB_Z, z_dev(to), RINGS[TAB_Z] + z)
+
     @pl.when(z == 1)
     def _():
         lax.fori_loop(0, owners, enter, 0)
 
-    arrived(FEAT_X)
-    for j in range(1, nx):
+    for j in sorted(range(1, nx), key=lambda j: min(j, nx - j)):
         slab = fbuf.at[core * nx + lax.rem(x + j, nx)]
+        wait(slab, recv.at[RINGS[FEAT_X] + lax.rem(x + j, nx)])
         put(slab, slab, FEAT_C, h_dev(x * 2 + 1 - core))
     expect(FEAT_C, fbuf.at[pl.ds(0, nx)], fbuf.at[pl.ds(0, nx)])
 
@@ -459,7 +457,7 @@
     for k in range(1, nh):
         put(norm.at[hd], norm.at[hd], NORM, h_dev(lax.rem(hd + k, nh)))
     expect(NORM, norm.at[pl.ds(0, nh - 1)], norm.at[pl.ds(0, nh - 1)])
-    arrived(NORM)
+    finish()
     square_sum = norm[0]
     for k in range(1, nh):
         square_sum = square_sum + norm[k]
@@ -468,8 +466,6 @@
     for h in range(NY):
         at = lanes(h)
         out[:, at] = (mixed[:, at] * scale * gain[:, at]).astype(BF16)
-
-    finish()
 
 
 def hbm(a):

time: 47.5 us -> 47.4 us (level)
  no operation moved by 1% of the time
where the time goes in v4:
time: 47.4 us; the launch traced here: 47.3 us
  Pallas kernels  46.5 us (98%)
  local copies, waits for them, and re-layouts  0.71 us (1%)
    pallas_call x1, Pallas kernels, local(): pl.pallas_call(functools.partial(kernel, nz, nh, inner * nh), out_shape=j...  46.5 us

profile of v4, /device:TPU:1, one launch (start us, length us, event | category | flops | bytes accessed | tf_op | source)
XLA Modules:
  0.0 47.3 jit_solution(17518319416498017228)
XLA Ops:
  0.0 46.5 %lightning.1 = bf16[128,1024]{1,0:T(8,128)(2,1)S(1)} custom-call(bf16[3,128,1024]{2,1,0:T(8,128)(2,1)} %bitcast.5, bf16[4,1024]{1,0:T(4,128)(2,1)} %feats_in.1, bf16[3,1024,1024]{2,1,0:T(8,128)(2,1)} %bitcast.4, s32[1,128]{1,0:T(1,128)} %bitcast.7, f32[8,128]{1,0:T(8,128)} %log_decay_in.1, f32[1,1024]{1,0:T(1,128)} %bitcast.6), custom_call_target="tpu_custom_call" | custom-call | tf_op jit(solution)/shard_map/lightning/pallas_call | solution.py:519
  46.6 0.7 %copy.8 = bf16[128,1024]{1,0:T(8,128)(2,1)} copy(bf16[128,1024]{1,0:T(8,128)(2,1)S(1)} %lightning.1) | data formatting | bytes 524288

commit v5 on v4

--- a/solution.py
+++ b/solution.py
@@ -34,7 +34,7 @@
 def kernel(
     nz, nh, heads_total,
     text_in, feats_in, w_in, vis_src_in, log_decay_in, gain_in, out,
-    text, feats, w, vis_src, log_decay, gain, ybuf, fbuf, kv_sum, query_sum, kv_all, query_all, s_out, s_in, e_out, e_in, pstate,
+    text, feats, w, vis_src, log_decay, gain, ybuf, fbuf, kv_sum, query_sum, query_all, s_out, s_in, e_out, e_in, pstate,
     t_out, t_in, r_out, r_in, raw, tot, tot_z, pre, tab_z, weight, factor, grown, mixed, norm,
     send, recv, load,
 ):
@@ -423,27 +423,21 @@
     arrived(FEAT_C)
     far_side, far_rows = feature_half(1 - core)
     mask = jnp.concatenate([is_vis] * (chunk // T), axis=1)
-    for m in range(2):
-        for start in range(0, inner, chunk):
-            cols = pl.ds(start, chunk)
-            visual = (kv_sum[m, :, cols] + dot(far_side, w[m + 1, far_rows, cols])).astype(BF16)
-            kv_all[m, :vr, cols] = visual
-            own = jnp.where(mask, dot(pick, visual), text[m + 1, :, cols].astype(F32))
-            kv_all[m, vr:, cols] = own.astype(BF16)
     placed = dot(pick, far_side).astype(BF16)
     for start in range(0, inner, chunk):
         cols = pl.ds(start, chunk)
+        keys_values = []
+        for m in range(2):
+            visual = (kv_sum[m, :, cols] + dot(far_side, w[m + 1, far_rows, cols])).astype(BF16)
+            own = jnp.where(mask, dot(pick, visual), text[m + 1, :, cols].astype(F32)).astype(BF16)
+            keys_values.append(jnp.concatenate([visual, own], axis=0))
         query = (query_sum[:, cols] + dot(placed, w[0, far_rows, cols])).astype(BF16).astype(F32)
-        query_all[:, cols] = jnp.where(mask, query, text[0, :, cols].astype(F32)).astype(BF16)
-
-    def head_within(h):
-        at = lanes(h)
-        query = query_all[:, at]
-        weights = dot(query, kv_all[0, :, at], ((1,), (1,))) * factor[h]
-        mixed[:, at] = dot(weights.astype(BF16), kv_all[1, :, at])
-
-    for h in range(NY):
-        head_within(h)
+        query = jnp.where(mask, query, text[0, :, cols].astype(F32)).astype(BF16)
+        query_all[:, cols] = query
+        for h in range(start // T, (start + chunk) // T):
+            at = slice(h * T - start, (h + 1) * T - start)
+            weights = dot(query[:, at], keys_values[0][:, at], ((1,), (1,))) * factor[h]
+            mixed[:, lanes(h)] = dot(weights.astype(BF16), keys_values[1][:, at])
 
     arrived(BACK_Y)
     squares = jnp.zeros((T, T), F32)
@@ -491,7 +485,6 @@
         pltpu.VMEM((nh, nz, 4 * NY, width // nh), BF16),
         pltpu.VMEM((2, vr, inner), F32),
         pltpu.VMEM((row_count, inner), F32),
-        pltpu.VMEM((2, vr + row_count, inner), BF16),
         pltpu.VMEM((row_count, inner), BF16),
         pltpu.VMEM((NY, T, T), BF16),
         pltpu.VMEM((NY, T, T), BF16),

time: 47.4 us -> 46.9 us (0.989)
  Pallas kernels: 46.5 us -> 46 us
    pallas_call x1, Pallas kernels: 46.5 us -> 46 us  [local(): pl.pallas_call(functools.partial(kernel, nz, nh, inner * nh), out_shape=j...]
where the time goes in v5:
time: 46.9 us; the launch traced here: 46.7 us
  Pallas kernels  46 us (98%)
  local copies, waits for them, and re-layouts  0.71 us (2%)
    pallas_call x1, Pallas kernels, local(): pl.pallas_call(functools.partial(kernel, nz, nh, inner * nh), out_shape=j...  46 us

profile of v5, /device:TPU:1, one launch (start us, length us, event | category | flops | bytes accessed | tf_op | source)
XLA Modules:
  0.0 46.7 jit_solution(7711753004038261190)
XLA Ops:
  0.0 46.0 %lightning.1 = bf16[128,1024]{1,0:T(8,128)(2,1)S(1)} custom-call(bf16[3,128,1024]{2,1,0:T(8,128)(2,1)} %bitcast.5, bf16[4,1024]{1,0:T(4,128)(2,1)} %feats_in.1, bf16[3,1024,1024]{2,1,0:T(8,128)(2,1)} %bitcast.4, s32[1,128]{1,0:T(1,128)} %bitcast.7, f32[8,128]{1,0:T(8,128)} %log_decay_in.1, f32[1,1024]{1,0:T(1,128)} %bitcast.6), custom_call_target="tpu_custom_call" | custom-call | tf_op jit(solution)/shard_map/lightning/pallas_call | solution.py:512
  46.0 0.7 %copy.8 = bf16[128,1024]{1,0:T(8,128)(2,1)} copy(bf16[128,1024]{1,0:T(8,128)(2,1)S(1)} %lightning.1) | data formatting | bytes 524288
